TPU v7x, 32 devices: a whole 2x2x4 slice. The times are simulated.
32 devices in a mesh: group: 8 (over z, y), tp: 4 (over x, core).
Axes of the slice: x: 2, y: 2, z: 4, core: 2. Of those that a mesh axis runs over, the one named last changes fastest.
Arguments:
- pf_query: bfloat16 [2048, 8192], P('group', 'tp'), may hold values from -16 to 16
- pf_cache: bfloat16 [8, 2, 4096, 1024], P('group', None, 'tp'), may hold values from -16 to 16
- pf_offset: int32 [8], replicated, may hold values from 0 to 3840
- dec_query: bfloat16 [16, 8192], P('group', 'tp'), may hold values from -16 to 16
- dec_cache: bfloat16 [24, 2, 2048, 1024], P('group', None, 'tp'), may hold values from -16 to 16
- slot_owner: int32 [24], replicated, may hold values from 0 to 15, as said below
- slot_len: int32 [24], replicated, may hold values from 1 to 2048
Outputs:
- pf_out: bfloat16 [2048, 8192], P('group', 'tp')
- dec_out: bfloat16 [16, 8192], P('group', 'tp')
Inputs may be any that keep to these rules, and one draw needn't show every extreme that they name: `slot_owner`: every decode request owns one or two slots.
All inputs are finite; a program needn't handle non-finite values.
Results may differ from a plain program's by a relative error of at most 0.005.
Values may be sent and summed in bfloat16 or wider, within the bound.
A program may use at most 128 MiB of HBM per device.

v0:
```python
import jax
import jax.numpy as jnp
from jax import lax
from jax.sharding import PartitionSpec as P

QH = 64
KVH = 8
HD = 128
negative_big = -1e30


def merged_2(value, axis, join):
    pieces = jax.tree.map(lambda part: lax.all_gather(part, axis), value)
    head = jax.tree.map(lambda part: part[0], pieces)
    tail = jax.tree.map(lambda part: part[1:], pieces)
    running, _ = lax.scan(lambda running, share: (join(running, share), None), head, tail)
    return running


def attend_block(queries, cache_keys, cache_values, visible, score_scale):
    scores = (
        jnp.einsum("qgd,nd->gqn", queries, cache_keys, preferred_element_type=jnp.float32)
        * score_scale
    )
    scores = jnp.where(visible[None], scores, negative_big)
    maxima = jnp.max(scores, axis=-1)
    weights = jnp.where(visible[None], jnp.exp(scores - maxima[..., None]), 0.0).astype(
        jnp.bfloat16
    )
    totals = jnp.sum(weights, axis=-1, dtype=jnp.float32)
    weighted = jnp.einsum("gqn,nd->gqd", weights, cache_values, preferred_element_type=jnp.float32)
    return (maxima, totals, weighted)


def merge_along(maxima, totals, weighted, axis):
    largest = jnp.max(maxima, axis=axis, keepdims=True)
    factor = jnp.exp(maxima - largest)
    return (
        jnp.squeeze(largest, axis),
        jnp.sum(totals * factor, axis=axis),
        jnp.sum(weighted * factor[..., None], axis=axis),
    )


def combine_pair(first, second):
    largest = jnp.maximum(first[0], second[0])
    first_factor = jnp.exp(first[0] - largest)
    second_factor = jnp.exp(second[0] - largest)
    return (
        largest,
        first[1] * first_factor + second[1] * second_factor,
        first[2] * first_factor[..., None] + second[2] * second_factor[..., None],
    )


def masked_merge(hits, maxima, totals, weighted):
    selected_picks = jnp.where(hits[:, :, None], maxima[None], negative_big)
    largest = jnp.max(selected_picks, axis=1)
    factor = jnp.where(hits[:, :, None], jnp.exp(selected_picks - largest[:, None]), 0.0)
    denominator = jnp.einsum("abh,bh->ah", factor, totals, precision=lax.Precision.HIGHEST)
    numerator = jnp.einsum("abh,bhd->ahd", factor, weighted, precision=lax.Precision.HIGHEST)
    return (largest, denominator, numerator)


def on_device(pf_query, pf_cache, pf_offset, dec_query, dec_cache, slot_owner, slot_len):
    tp_count = lax.axis_size("tp")
    tp_rank = lax.axis_index("tp")
    group_rank = lax.axis_index("group")
    head_size = HD
    kv_heads = KVH
    width = QH // KVH
    local_heads = QH // tp_count
    score_scale = head_size ** (-0.5)
    pf_rows = pf_query.shape[0]
    local_len = pf_cache.shape[2]
    offset = lax.dynamic_index_in_dim(pf_offset, group_rank, keepdims=False)
    query_pos = offset + jnp.arange(pf_rows, dtype=jnp.int32)
    every_head = lax.all_gather(pf_query, "tp", axis=1, tiled=True)
    grouped = jnp.moveaxis(every_head.reshape(pf_rows, kv_heads, width, head_size), 1, 0)
    cache_keys = jnp.moveaxis(pf_cache[0, 0].reshape(local_len, kv_heads, head_size), 1, 0)
    cache_values = jnp.moveaxis(pf_cache[0, 1].reshape(local_len, kv_heads, head_size), 1, 0)
    key_pos = tp_rank * local_len + jnp.arange(local_len, dtype=jnp.int32)
    visible = key_pos[None, :] <= query_pos[:, None]
    maxima, totals, weighted = lax.map(
        lambda items: attend_block(items[0], items[1], items[2], visible, score_scale),
        (grouped, cache_keys, cache_values),
    )
    maxima = maxima.reshape(tp_count, local_heads, pf_rows)
    totals = totals.reshape(tp_count, local_heads, pf_rows)
    weighted = weighted.reshape(tp_count, local_heads, pf_rows, head_size)
    maxima, totals, weighted = (
        lax.all_to_all(maxima, "tp", split_axis=0, concat_axis=0, tiled=True),
        lax.all_to_all(totals, "tp", split_axis=0, concat_axis=0, tiled=True),
        lax.all_to_all(weighted, "tp", split_axis=0, concat_axis=0, tiled=True),
    )
    largest, denominator, numerator = merge_along(maxima, totals, weighted, 0)
    prefill_heads = numerator / denominator[..., None]
    pf_out = (
        jnp.moveaxis(prefill_heads, 1, 0)
        .reshape(pf_rows, local_heads * head_size)
        .astype(jnp.bfloat16)
    )
    served = dec_query.shape[0]
    head_queries_dec = lax.all_gather(dec_query, "tp", axis=1, tiled=True)
    all_queries = lax.all_gather(head_queries_dec, "group", axis=0, tiled=True)
    slots_here = dec_cache.shape[0]
    slot_local_len = dec_cache.shape[2]
    owners = lax.dynamic_slice_in_dim(slot_owner, group_rank * slots_here, slots_here)
    length_list = lax.dynamic_slice_in_dim(slot_len, group_rank * slots_here, slots_here)
    slot_queries = jnp.take(all_queries, owners, axis=0).reshape(
        slots_here, kv_heads, width, head_size
    )
    slot_keys = dec_cache[:, 0].reshape(slots_here, slot_local_len, kv_heads, head_size)
    slot_values = dec_cache[:, 1].reshape(slots_here, slot_local_len, kv_heads, head_size)
    scores = (
        jnp.einsum("skgd,slkd->skgl", slot_queries, slot_keys, preferred_element_type=jnp.float32)
        * score_scale
    )
    slot_pos = tp_rank * slot_local_len + jnp.arange(slot_local_len, dtype=jnp.int32)
    live = (slot_pos[None, :] < length_list[:, None])[:, None, None, :]
    scores = jnp.where(live, scores, negative_big)
    slot_max = jnp.max(scores, axis=-1)
    slot_weights = jnp.where(live, jnp.exp(scores - slot_max[..., None]), 0.0).astype(jnp.bfloat16)
    slot_totals = jnp.sum(slot_weights, axis=-1, dtype=jnp.float32)
    slot_weighted = jnp.einsum(
        "skgl,slkd->skgd", slot_weights, slot_values, preferred_element_type=jnp.float32
    )
    slot_max = slot_max.reshape(slots_here, QH)
    slot_totals = slot_totals.reshape(slots_here, QH)
    slot_weighted = slot_weighted.reshape(slots_here, QH, head_size)
    merged = merged_2((slot_max, slot_totals, slot_weighted), "tp", combine_pair)
    head_max = lax.dynamic_slice_in_dim(merged[0], tp_rank * local_heads, local_heads, 1)
    head_totals = lax.dynamic_slice_in_dim(merged[1], tp_rank * local_heads, local_heads, 1)
    head_weighted = lax.dynamic_slice_in_dim(merged[2], tp_rank * local_heads, local_heads, 1)
    every_max, every_totals, every_weighted = (
        lax.all_gather(head_max, "group", axis=0, tiled=True),
        lax.all_gather(head_totals, "group", axis=0, tiled=True),
        lax.all_gather(head_weighted, "group", axis=0, tiled=True),
    )
    mine = group_rank * served + jnp.arange(served, dtype=jnp.int32)
    hits = slot_owner[None, :] == mine[:, None]
    largest_dec, denominator_dec, numerator_dec = masked_merge(
        hits, every_max, every_totals, every_weighted
    )
    dec_out = (
        (numerator_dec / denominator_dec[..., None])
        .reshape(served, local_heads * head_size)
        .astype(jnp.bfloat16)
    )
    return (pf_out, dec_out)


def solution(mesh):
    placed = (
        P("group", "tp"),
        P("group", None, "tp", None),
        P(),
        P("group", "tp"),
        P("group", None, "tp", None),
        P(),
        P(),
    )
    return jax.shard_map(
        on_device,
        mesh=mesh,
        in_specs=placed,
        out_specs=(P("group", "tp"), P("group", "tp")),
        check_vma=False,
    )
```

profile of v0, /device:TPU:0, one launch (start us, length us, event | category | flops | bytes accessed | tf_op | source)
XLA Modules:
  0.0 403.5 jit_solution(4472428663473686276)
XLA Ops:
  7.2 2.3 copy.40
  9.5 4.0 fusion.46
  13.5 4.0 copy.61
  17.5 2.6 copy.62
  21.2 26.1 %all-gather.5.cloned.1.call-done = bf16[256,8192]{0,1:T(8,128)(2,1)} async-done(((bf16[256,2048]{0,1:T(8,128)(2,1)}), bf16[256,8192]{0,1:T(8,128)(2,1)}) %all-gather.5.cloned.1.call-update) | async-done | bytes 4194320 | tf_op jit(solution)/shard_map/all_gather | solution.py:78
  47.3 74.8 %while.30 = (s32[]{:T(128)}, f32[8,8,256]{2,1,0:T(8,128)S(1)}, f32[8,8,256]{2,1,0:T(8,128)S(1)}, f32[8,8,256,128]{3,2,1,0:T(8,128)}, bf16[8,1024,128]{1,2,0:T(8,...) while((s32[]{:T(128)}, f32[8,8,256]{2,1,0:T(8,128)S(1)}, ...), condition=%wide.region_3.4_spmd.clone, body=%wide.region_0.3_spmd.clone.sunk | while | flops 1105457152 | bytes 28384368 | solution.py:84
  47.6 2.6 fusion.59
  50.2 2.0 convert_reduce_fusion.3
  52.2 4.6 %fusion.60 = f32[8,8,256,128]{3,2,1,0:T(8,128)} fusion(f32[8,8,256,128]{3,2,1,0:T(8,128)} %get-tuple-element.319, s32[]{:T(128)S(6)} %copy.81, bf16[8,1024,128]{1,2,0:T(8,128)(2,1)} %get-tuple-element.332, f32[1024,256,8]{1,0,2:T(8,128)S(1)} %get-tuple-element.303, f32[8,256]{1,0:T(8,128)S(1)} %get-tuple-element.302, ...), kind=kOutput, calls=%fused_computation.15.clone.1 | convolution fusion | flops 547356672 | bytes 9970688 | tf_op jit(solution)/shard_map/while/body/eval_jaxpr/gqn,nd->gqd/dot_general | solution.py:31
  57.0 2.6 fusion.59
  59.6 2.0 convert_reduce_fusion.3
  61.6 4.5 %fusion.60 = f32[8,8,256,128]{3,2,1,0:T(8,128)} fusion(f32[8,8,256,128]{3,2,1,0:T(8,128)} %get-tuple-element.319, s32[]{:T(128)S(6)} %copy.81, bf16[8,1024,128]{1,2,0:T(8,128)(2,1)} %get-tuple-element.332, f32[1024,256,8]{1,0,2:T(8,128)S(1)} %get-tuple-element.303, f32[8,256]{1,0:T(8,128)S(1)} %get-tuple-element.302, ...), kind=kOutput, calls=%fused_computation.15.clone.1 | convolution fusion | flops 547356672 | bytes 9970688 | tf_op jit(solution)/shard_map/while/body/eval_jaxpr/gqn,nd->gqd/dot_general | solution.py:31
  66.3 2.6 fusion.59
  68.9 2.0 convert_reduce_fusion.3
  70.9 4.5 %fusion.60 = f32[8,8,256,128]{3,2,1,0:T(8,128)} fusion(f32[8,8,256,128]{3,2,1,0:T(8,128)} %get-tuple-element.319, s32[]{:T(128)S(6)} %copy.81, bf16[8,1024,128]{1,2,0:T(8,128)(2,1)} %get-tuple-element.332, f32[1024,256,8]{1,0,2:T(8,128)S(1)} %get-tuple-element.303, f32[8,256]{1,0:T(8,128)S(1)} %get-tuple-element.302, ...), kind=kOutput, calls=%fused_computation.15.clone.1 | convolution fusion | flops 547356672 | bytes 9970688 | tf_op jit(solution)/shard_map/while/body/eval_jaxpr/gqn,nd->gqd/dot_general | solution.py:31
  75.6 2.6 fusion.59
  78.2 2.0 convert_reduce_fusion.3
  80.3 4.5 %fusion.60 = f32[8,8,256,128]{3,2,1,0:T(8,128)} fusion(f32[8,8,256,128]{3,2,1,0:T(8,128)} %get-tuple-element.319, s32[]{:T(128)S(6)} %copy.81, bf16[8,1024,128]{1,2,0:T(8,128)(2,1)} %get-tuple-element.332, f32[1024,256,8]{1,0,2:T(8,128)S(1)} %get-tuple-element.303, f32[8,256]{1,0:T(8,128)S(1)} %get-tuple-element.302, ...), kind=kOutput, calls=%fused_computation.15.clone.1 | convolution fusion | flops 547356672 | bytes 9970688 | tf_op jit(solution)/shard_map/while/body/eval_jaxpr/gqn,nd->gqd/dot_general | solution.py:31
  84.9 2.6 fusion.59
  87.5 2.0 convert_reduce_fusion.3
  89.6 4.5 %fusion.60 = f32[8,8,256,128]{3,2,1,0:T(8,128)} fusion(f32[8,8,256,128]{3,2,1,0:T(8,128)} %get-tuple-element.319, s32[]{:T(128)S(6)} %copy.81, bf16[8,1024,128]{1,2,0:T(8,128)(2,1)} %get-tuple-element.332, f32[1024,256,8]{1,0,2:T(8,128)S(1)} %get-tuple-element.303, f32[8,256]{1,0:T(8,128)S(1)} %get-tuple-element.302, ...), kind=kOutput, calls=%fused_computation.15.clone.1 | convolution fusion | flops 547356672 | bytes 9970688 | tf_op jit(solution)/shard_map/while/body/eval_jaxpr/gqn,nd->gqd/dot_general | solution.py:31
  94.3 2.6 fusion.59
  96.9 2.0 convert_reduce_fusion.3
  99.0 4.5 %fusion.60 = f32[8,8,256,128]{3,2,1,0:T(8,128)} fusion(f32[8,8,256,128]{3,2,1,0:T(8,128)} %get-tuple-element.319, s32[]{:T(128)S(6)} %copy.81, bf16[8,1024,128]{1,2,0:T(8,128)(2,1)} %get-tuple-element.332, f32[1024,256,8]{1,0,2:T(8,128)S(1)} %get-tuple-element.303, f32[8,256]{1,0:T(8,128)S(1)} %get-tuple-element.302, ...), kind=kOutput, calls=%fused_computation.15.clone.1 | convolution fusion | flops 547356672 | bytes 9970688 | tf_op jit(solution)/shard_map/while/body/eval_jaxpr/gqn,nd->gqd/dot_general | solution.py:31
  103.7 2.6 fusion.59
  106.3 2.0 convert_reduce_fusion.3
  108.3 4.5 %fusion.60 = f32[8,8,256,128]{3,2,1,0:T(8,128)} fusion(f32[8,8,256,128]{3,2,1,0:T(8,128)} %get-tuple-element.319, s32[]{:T(128)S(6)} %copy.81, bf16[8,1024,128]{1,2,0:T(8,128)(2,1)} %get-tuple-element.332, f32[1024,256,8]{1,0,2:T(8,128)S(1)} %get-tuple-element.303, f32[8,256]{1,0:T(8,128)S(1)} %get-tuple-element.302, ...), kind=kOutput, calls=%fused_computation.15.clone.1 | convolution fusion | flops 547356672 | bytes 9970688 | tf_op jit(solution)/shard_map/while/body/eval_jaxpr/gqn,nd->gqd/dot_general | solution.py:31
  113.0 2.6 fusion.59
  115.6 2.0 convert_reduce_fusion.3
  117.6 4.5 %fusion.60 = f32[8,8,256,128]{3,2,1,0:T(8,128)} fusion(f32[8,8,256,128]{3,2,1,0:T(8,128)} %get-tuple-element.319, s32[]{:T(128)S(6)} %copy.81, bf16[8,1024,128]{1,2,0:T(8,128)(2,1)} %get-tuple-element.332, f32[1024,256,8]{1,0,2:T(8,128)S(1)} %get-tuple-element.303, f32[8,256]{1,0:T(8,128)S(1)} %get-tuple-element.302, ...), kind=kOutput, calls=%fused_computation.15.clone.1 | convolution fusion | flops 547356672 | bytes 9970688 | tf_op jit(solution)/shard_map/while/body/eval_jaxpr/gqn,nd->gqd/dot_general | solution.py:31
  122.1 7.1 %all_to_all.15 = f32[4,16,256]{2,1,0:T(8,128)} all-to-all(f32[4,16,256]{2,1,0:T(8,128)S(1)} %bitcast.139), channel_id=1, replica_groups=mesh['group'=8,'tp'=4] {'tp'}, dimensions={0} | all-to-all | bytes 131072 | tf_op jit(solution)/shard_map/all_to_all | solution.py:93
  129.2 7.1 %all_to_all.16 = f32[4,16,256]{2,1,0:T(8,128)} all-to-all(f32[4,16,256]{2,1,0:T(8,128)S(1)} %bitcast.138), channel_id=1, replica_groups=mesh['group'=8,'tp'=4] {'tp'}, dimensions={0} | all-to-all | bytes 131072 | tf_op jit(solution)/shard_map/all_to_all | solution.py:92
  136.4 5.7 %all-to-all-start = ((f32[4,16,256,128]{3,2,1,0:T(8,128)}), f32[4,16,256,128]{3,2,1,0:T(8,128)}, u32[]{:S(2)}, u32[]{:S(2)}) async-start(f32[4,16,256,128]{3,2,1,0:T(8,128)} %bitcast.130), calls=%async_computation | async-start | bytes 16777216 | tf_op jit(solution)/shard_map/all_to_all | solution.py:94
  142.1 6.9 %fusion.45 = (bf16[3,1,512,1024]{3,2,1,0:T(8,128)(2,1)}, bf16[3,1,512,1024]{3,2,1,0:T(8,128)(2,1)}) fusion(bf16[3,2,512,1024]{3,2,1,0:T(8,128)(2,1)} %param.15), kind=kLoop, calls=%fused_computation.81 | loop fusion | bytes 12582912 | tf_op jit(solution)/shard_map/slice | solution.py:114
  149.0 3.2 copy.63
  152.2 84.0 %all_gather.28 = bf16[2,8192]{1,0:T(2,128)(2,1)S(1)} all-gather(bf16[2,2048]{1,0:T(2,128)(2,1)S(1)} %copy-done.2), channel_id=1, replica_groups=mesh['group'=8,'tp'=4] {'tp'}, dimensions={1}, use_global_device_ids=true | all-gather | bytes 40960 | tf_op jit(solution)/shard_map/all_gather | solution.py:104
  236.2 32.8 %all-gather = bf16[8,2,8192]{2,1,0:T(2,128)(2,1)} all-gather(bf16[1,2,8192]{2,1,0:T(2,128)(2,1)S(1)} %bitcast.136), channel_id=1, replica_groups=mesh['group'=8,'tp'=4] {'group'}, dimensions={0}, use_global_device_ids=true | all-gather | bytes 294912 | tf_op jit(solution)/shard_map/all_gather | solution.py:105
  272.0 1.5 fusion.47
  275.1 3.2 copy.64
  278.3 5.3 %all_gather.30 = f32[4,3,64]{2,1,0:T(4,128)S(1)} all-gather(f32[1,3,64]{2,1,0:T(4,128)} %all_gather_reshape.9), channel_id=1, replica_groups=mesh['group'=8,'tp'=4] {'tp'}, dimensions={0}, use_global_device_ids=true | all-gather | bytes 3840 | tf_op jit(solution)/shard_map/all_gather | solution.py:13
  284.2 5.3 %all_gather.31 = f32[4,3,64]{2,1,0:T(4,128)S(1)} all-gather(f32[1,3,64]{2,1,0:T(4,128)} %all_gather_reshape.10), channel_id=1, replica_groups=mesh['group'=8,'tp'=4] {'tp'}, dimensions={0}, use_global_device_ids=true | all-gather | bytes 3840 | tf_op jit(solution)/shard_map/all_gather | solution.py:13
  291.0 6.5 %all_gather.32 = f32[4,3,64,128]{3,2,1,0:T(8,128)S(1)} all-gather(f32[1,3,64,128]{3,2,1,0:T(8,128)S(1)} %convolution_bitcast_fusion.1), channel_id=1, replica_groups=mesh['group'=8,'tp'=4] {'tp'}, dimensions={0}, use_global_device_ids=true | all-gather | bytes 491520 | tf_op jit(solution)/shard_map/all_gather | solution.py:13
  298.9 2.6 while.29
  301.6 26.0 %all-gather.2 = f32[8,3,16]{2,1,0:T(4,128)S(1)} all-gather(f32[1,3,16]{2,1,0:T(4,128)S(1)} %dynamic-slice_bitcast_fusion), channel_id=1, replica_groups=mesh['group'=8,'tp'=4] {'group'}, dimensions={0}, use_global_device_ids=true | all-gather | bytes 1728 | tf_op jit(solution)/shard_map/all_gather | solution.py:137
  327.8 26.2 %all-gather.1 = f32[8,3,16]{2,1,0:T(4,128)S(1)} all-gather(f32[1,3,16]{2,1,0:T(4,128)S(1)} %dynamic-slice_bitcast_fusion.1), channel_id=1, replica_groups=mesh['group'=8,'tp'=4] {'group'}, dimensions={0}, use_global_device_ids=true | all-gather | bytes 1728 | tf_op jit(solution)/shard_map/all_gather | solution.py:136
  354.0 30.6 %all_gather.33 = f32[24,16,128]{2,1,0:T(8,128)S(1)} all-gather(f32[3,16,128]{2,1,0:T(8,128)S(1)} %constant_dynamic-slice_fusion), channel_id=1, replica_groups=mesh['group'=8,'tp'=4] {'group'}, dimensions={0}, use_global_device_ids=true | all-gather | bytes 221184 | tf_op jit(solution)/shard_map/all_gather | solution.py:138
  388.5 5.4 %multiply_reduce_fusion = f32[16,256,128]{2,1,0:T(8,128)S(1)} fusion(f32[4,16,256,128]{3,2,1,0:T(8,128)} %all-to-all-done, f32[4,16,256]{2,1,0:T(8,128)S(1)} %get-tuple-element.181), kind=kLoop, calls=%fused_computation.28 | loop fusion | flops 3670016 | bytes 10551296 | tf_op jit(solution)/shard_map/reduce_sum | solution.py:41
  395.2 1.4 copy.52
  (76 shorter events, 19.0 us)
Async XLA Ops:
  7.2 40.2 %all-gather.5.cloned.1.call-start = ((), (), s32[]{:S(2)}) async-start(), calls=%async_computation.3 | async-start | bytes 5242880 | tf_op jit(solution)/shard_map/all_gather | solution.py:78
  13.5 6.5 %copy-start.4 = (s32[8]{0:T(128)S(1)}, s32[8]{0:T(128)}, u32[]{:S(2)}) copy-start(s32[8]{0:T(128)} %param.13) | copy-start | bytes 100
  136.4 252.1 %all-to-all-start = ((f32[4,16,256,128]{3,2,1,0:T(8,128)}), f32[4,16,256,128]{3,2,1,0:T(8,128)}, u32[]{:S(2)}, u32[]{:S(2)}) async-start(f32[4,16,256,128]{3,2,1,0:T(8,128)} %bitcast.130), calls=%async_computation | async-start | bytes 16777216 | tf_op jit(solution)/shard_map/all_to_all | solution.py:94
  149.0 3.2 copy-start.2
  149.0 121.1 %copy-start.5 = (s32[24]{0:T(128)S(1)}, s32[24]{0:T(128)}, u32[]{:S(2)}) copy-start(s32[24]{0:T(128)} %param.17) | copy-start | bytes 292
  149.0 121.2 %copy-start.3 = (s32[24]{0:T(128)S(1)}, s32[24]{0:T(128)}, u32[]{:S(2)}) copy-start(s32[24]{0:T(128)} %param.16) | copy-start | bytes 292
  283.6 6.5 %copy-start = (f32[4,3,64]{2,1,0:T(4,128)}, f32[4,3,64]{2,1,0:T(4,128)S(1)}, u32[]{:S(2)}) copy-start(f32[4,3,64]{2,1,0:T(4,128)S(1)} %all_gather.30) | copy-start | bytes 9220
  289.4 0.6 copy-start.1
Sparse Core Ops, SparseCore 0:
  10.1 37.1 all-gather.4
where the time goes:
time: 405 us; the launch traced here: 403 us
  blocking collectives  231 us (57%)
  matrix products  60.3 us (15%)
  local copies, waits for them, and re-layouts  35.3 us (9%)
  other arithmetic  30.4 us (8%)
  waiting for transfers between devices  26.1 us (6%)
  between operations  14.2 us (4%)
  starting transfers between devices  5.69 us (1%)
    all_gather x1, blocking collectives, on_device(): head_queries_dec = lax.all_gather(dec_query, 'tp', axis=1, tiled=True)  84 us
    dot_general x8, matrix products, attend_block(): jnp.einsum('gqn,nd->gqd', weights, cache_values, preferred_element_type=j...  35.9 us
    all_gather x1, blocking collectives, on_device(): all_queries = lax.all_gather(head_queries_dec, 'group', axis=0, tiled=True)  32.8 us
    all_gather x1, blocking collectives, on_device(): lax.all_gather(head_weighted, 'group', axis=0, tiled=True)  30.6 us
    all_gather x1, blocking collectives, on_device(): lax.all_gather(head_max, 'group', axis=0, tiled=True)  26.2 us
    all_gather x1, waiting for transfers between devices, on_device(): every_head = lax.all_gather(pf_query, 'tp', axis=1, tiled=True)  26.1 us
    all_gather x1, blocking collectives, on_device(): lax.all_gather(head_totals, 'group', axis=0, tiled=True)  26 us
    dot_general x8, matrix products, attend_block(): jnp.einsum('qgd,nd->gqn', queries, cache_keys, preferred_element_type=jnp...  20.8 us
  transfers between devices with their start and end apart: 2, of which 1 were waited for; matrix products, arithmetic and copies ran while one was open for 10% of the time, Pallas kernels for 0%

commit v1 on v0

--- a/solution.py
+++ b/solution.py
@@ -101,7 +101,17 @@
         .astype(jnp.bfloat16)
     )
     served = dec_query.shape[0]
-    head_queries_dec = lax.all_gather(dec_query, "tp", axis=1, tiled=True)
+    dev_n = lax.axis_size("tp")
+    nodes = [dec_query]
+    for i in range(dev_n - 1):
+        nodes.append(
+            lax.ppermute(
+                nodes[-1], axis_name="tp", perm=[(w, (w + 1) % dev_n) for w in range(dev_n)]
+            )
+        )
+    head_queries_dec = jnp.roll(
+        jnp.concatenate(nodes[::-1], 1), (lax.axis_index("tp") + 1) * dec_query.shape[1], 1
+    )
     all_queries = lax.all_gather(head_queries_dec, "group", axis=0, tiled=True)
     slots_here = dec_cache.shape[0]
     slot_local_len = dec_cache.shape[2]

time: 405 us -> 360 us (0.89)
  blocking collectives: 231 us -> 184 us
  waiting for transfers between devices: 26.1 us -> 15.6 us
  starting transfers between devices: 5.69 us -> 15.8 us
    all_gather x1 -> x0, blocking collectives: 84 us -> none  [on_device(): head_queries_dec = lax.all_gather(dec_query, 'tp', axis=1, tiled=True)]
    all_gather x3, blocking collectives: 17.1 us -> 68.6 us  [merged_2(): pieces = jax.tree.map(lambda part: lax.all_gather(part, axis), value)]
    all_gather x1, waiting for transfers between devices: 26.1 us -> 7.45 us  [on_device(): every_head = lax.all_gather(pf_query, 'tp', axis=1, tiled=True)]
    all_to_all x2 -> x0, blocking collectives: 14.3 us -> none  [the longest x1 7.15 us: on_device(): lax.all_to_all(maxima, 'tp', split_axis=0, concat_axis=0, tiled=True)]
    all_to_all x0 -> x2, waiting for transfers between devices: none -> 8.13 us  [the longest x1 4.07 us: on_device(): lax.all_to_all(maxima, 'tp', split_axis=0, concat_axis=0, tiled=True)]
    all_to_all x0 -> x2, starting transfers between devices: none -> 6.56 us  [the longest x1 3.28 us: on_device(): lax.all_to_all(totals, 'tp', split_axis=0, concat_axis=0, tiled=True)]
    dynamic_update_slice x8, local copies, waits for them, and re-layouts: 0.07 us -> 4.88 us  [on_device(): lax.map(lambda items: attend_block(items[0], items[1], items[2], visible,...]
    unnamed x25 -> x37, local copies, waits for them, and re-layouts: 18 us -> 20.9 us
  transfers between devices with their start and end apart: 2 -> 7, of which waited for: 1 -> 3; matrix products, arithmetic and copies ran while one was open for 10% -> 33% of each run, Pallas kernels for 0% -> 0%
where the time goes in v1:
time: 360 us; the launch traced here: 359 us
  blocking collectives  184 us (51%)
  matrix products  62.8 us (17%)
  local copies, waits for them, and re-layouts  36.8 us (10%)
  other arithmetic  28.9 us (8%)
  starting transfers between devices  15.8 us (4%)
  waiting for transfers between devices  15.6 us (4%)
  between operations  14.3 us (4%)
    all_gather x3, blocking collectives, merged_2(): pieces = jax.tree.map(lambda part: lax.all_gather(part, axis), value)  68.6 us
    dot_general x8, matrix products, attend_block(): jnp.einsum('gqn,nd->gqd', weights, cache_values, preferred_element_type=j...  35.8 us
    all_gather x1, blocking collectives, on_device(): all_queries = lax.all_gather(head_queries_dec, 'group', axis=0, tiled=True)  32.8 us
    all_gather x1, blocking collectives, on_device(): lax.all_gather(head_weighted, 'group', axis=0, tiled=True)  30.6 us
    all_gather x1, blocking collectives, on_device(): lax.all_gather(head_totals, 'group', axis=0, tiled=True)  26.2 us
    all_gather x1, blocking collectives, on_device(): lax.all_gather(head_max, 'group', axis=0, tiled=True)  26 us
    unnamed x37, local copies, waits for them, and re-layouts  20.9 us
    dot_general x8, matrix products, attend_block(): jnp.einsum('qgd,nd->gqn', queries, cache_keys, preferred_element_type=jnp...  20.8 us
  transfers between devices with their start and end apart: 7, of which 3 were waited for; matrix products, arithmetic and copies ran while one was open for 33% of the time, Pallas kernels for 0%

profile of v1, /device:TPU:0, one launch (start us, length us, event | category | flops | bytes accessed | tf_op | source)
XLA Modules:
  0.0 358.6 jit_solution(10446828984978401989)
XLA Ops:
  7.2 2.3 copy.40
  13.7 4.0 %fusion.46 = (bf16[1,1,1024,1024]{3,2,1,0:T(8,128)(2,1)S(1)}, bf16[1,1,1024,1024]{3,2,1,0:T(8,128)(2,1)}) fusion(bf16[1,2,1024,1024]{3,2,1,0:T(8,128)(2,1)} %param.12), kind=kLoop, calls=%fused_computation.91 | loop fusion | bytes 8388608 | tf_op jit(solution)/shard_map/slice | solution.py:81
  17.7 3.5 fusion.45
  21.9 2.6 collective-permute-start.1
  25.2 4.0 %copy.61 = bf16[1,1,1024,1024]{2,3,1,0:T(8,128)(2,1)} copy(bf16[1,1,1024,1024]{3,2,1,0:T(8,128)(2,1)} %get-tuple-element.189) | data formatting | bytes 4194304
  29.2 2.6 copy.62
  31.7 3.2 copy.63
  34.9 4.7 %copy.64 = bf16[3,1,512,1024]{2,3,0,1:T(8,128)(2,1)} copy(bf16[3,1,512,1024]{3,2,1,0:T(8,128)(2,1)} %get-tuple-element.186) | data formatting | bytes 6291456
  40.1 7.5 %all-gather.5.cloned.1.call-done = bf16[256,8192]{0,1:T(8,128)(2,1)} async-done(((bf16[256,2048]{0,1:T(8,128)(2,1)}), bf16[256,8192]{0,1:T(8,128)(2,1)}) %all-gather.5.cloned.1.call-update) | async-done | bytes 4194320 | tf_op jit(solution)/shard_map/all_gather | solution.py:78
  47.5 79.4 %while.30 = (s32[]{:T(128)}, f32[8,8,256]{2,1,0:T(8,128)}, f32[8,8,256]{2,1,0:T(8,128)}, f32[8,8,256,128]{3,2,1,0:T(8,128)}, bf16[8,1024,128]{1,2,0:T(8,128)(2,1...) while((s32[]{:T(128)}, f32[8,8,256]{2,1,0:T(8,128)}, ...), condition=%wide.region_3.4_spmd.clone, body=%wide.region_0.3_spmd.clone.sunk | while | flops 1105457152 | bytes 28384368 | solution.py:84
  47.7 2.6 fusion.59
  50.3 2.0 convert_reduce_fusion.3
  53.0 4.5 %fusion.60 = f32[8,8,256,128]{3,2,1,0:T(8,128)} fusion(f32[8,8,256,128]{3,2,1,0:T(8,128)} %get-tuple-element.319, s32[]{:T(128)S(6)} %copy.81, bf16[8,1024,128]{1,2,0:T(8,128)(2,1)} %get-tuple-element.332, f32[1024,256,8]{1,0,2:T(8,128)S(1)} %get-tuple-element.303, f32[8,256]{1,0:T(8,128)S(1)} %get-tuple-element.302, ...), kind=kOutput, calls=%fused_computation.15.clone.1 | convolution fusion | flops 547356672 | bytes 9970688 | tf_op jit(solution)/shard_map/while/body/eval_jaxpr/gqn,nd->gqd/dot_general | solution.py:31
  57.7 2.6 fusion.59
  60.3 2.0 convert_reduce_fusion.3
  63.0 4.4 %fusion.60 = f32[8,8,256,128]{3,2,1,0:T(8,128)} fusion(f32[8,8,256,128]{3,2,1,0:T(8,128)} %get-tuple-element.319, s32[]{:T(128)S(6)} %copy.81, bf16[8,1024,128]{1,2,0:T(8,128)(2,1)} %get-tuple-element.332, f32[1024,256,8]{1,0,2:T(8,128)S(1)} %get-tuple-element.303, f32[8,256]{1,0:T(8,128)S(1)} %get-tuple-element.302, ...), kind=kOutput, calls=%fused_computation.15.clone.1 | convolution fusion | flops 547356672 | bytes 9970688 | tf_op jit(solution)/shard_map/while/body/eval_jaxpr/gqn,nd->gqd/dot_general | solution.py:31
  67.6 2.6 fusion.59
  70.2 2.0 convert_reduce_fusion.3
  72.9 4.4 %fusion.60 = f32[8,8,256,128]{3,2,1,0:T(8,128)} fusion(f32[8,8,256,128]{3,2,1,0:T(8,128)} %get-tuple-element.319, s32[]{:T(128)S(6)} %copy.81, bf16[8,1024,128]{1,2,0:T(8,128)(2,1)} %get-tuple-element.332, f32[1024,256,8]{1,0,2:T(8,128)S(1)} %get-tuple-element.303, f32[8,256]{1,0:T(8,128)S(1)} %get-tuple-element.302, ...), kind=kOutput, calls=%fused_computation.15.clone.1 | convolution fusion | flops 547356672 | bytes 9970688 | tf_op jit(solution)/shard_map/while/body/eval_jaxpr/gqn,nd->gqd/dot_general | solution.py:31
  77.5 2.6 fusion.59
  80.1 2.0 convert_reduce_fusion.3
  82.8 4.5 %fusion.60 = f32[8,8,256,128]{3,2,1,0:T(8,128)} fusion(f32[8,8,256,128]{3,2,1,0:T(8,128)} %get-tuple-element.319, s32[]{:T(128)S(6)} %copy.81, bf16[8,1024,128]{1,2,0:T(8,128)(2,1)} %get-tuple-element.332, f32[1024,256,8]{1,0,2:T(8,128)S(1)} %get-tuple-element.303, f32[8,256]{1,0:T(8,128)S(1)} %get-tuple-element.302, ...), kind=kOutput, calls=%fused_computation.15.clone.1 | convolution fusion | flops 547356672 | bytes 9970688 | tf_op jit(solution)/shard_map/while/body/eval_jaxpr/gqn,nd->gqd/dot_general | solution.py:31
  87.5 2.6 fusion.59
  90.1 2.0 convert_reduce_fusion.3
  92.7 4.5 %fusion.60 = f32[8,8,256,128]{3,2,1,0:T(8,128)} fusion(f32[8,8,256,128]{3,2,1,0:T(8,128)} %get-tuple-element.319, s32[]{:T(128)S(6)} %copy.81, bf16[8,1024,128]{1,2,0:T(8,128)(2,1)} %get-tuple-element.332, f32[1024,256,8]{1,0,2:T(8,128)S(1)} %get-tuple-element.303, f32[8,256]{1,0:T(8,128)S(1)} %get-tuple-element.302, ...), kind=kOutput, calls=%fused_computation.15.clone.1 | convolution fusion | flops 547356672 | bytes 9970688 | tf_op jit(solution)/shard_map/while/body/eval_jaxpr/gqn,nd->gqd/dot_general | solution.py:31
  97.4 2.6 fusion.59
  100.0 2.0 convert_reduce_fusion.3
  102.7 4.5 %fusion.60 = f32[8,8,256,128]{3,2,1,0:T(8,128)} fusion(f32[8,8,256,128]{3,2,1,0:T(8,128)} %get-tuple-element.319, s32[]{:T(128)S(6)} %copy.81, bf16[8,1024,128]{1,2,0:T(8,128)(2,1)} %get-tuple-element.332, f32[1024,256,8]{1,0,2:T(8,128)S(1)} %get-tuple-element.303, f32[8,256]{1,0:T(8,128)S(1)} %get-tuple-element.302, ...), kind=kOutput, calls=%fused_computation.15.clone.1 | convolution fusion | flops 547356672 | bytes 9970688 | tf_op jit(solution)/shard_map/while/body/eval_jaxpr/gqn,nd->gqd/dot_general | solution.py:31
  107.3 2.6 fusion.59
  109.9 2.0 convert_reduce_fusion.3
  112.6 4.5 %fusion.60 = f32[8,8,256,128]{3,2,1,0:T(8,128)} fusion(f32[8,8,256,128]{3,2,1,0:T(8,128)} %get-tuple-element.319, s32[]{:T(128)S(6)} %copy.81, bf16[8,1024,128]{1,2,0:T(8,128)(2,1)} %get-tuple-element.332, f32[1024,256,8]{1,0,2:T(8,128)S(1)} %get-tuple-element.303, f32[8,256]{1,0:T(8,128)S(1)} %get-tuple-element.302, ...), kind=kOutput, calls=%fused_computation.15.clone.1 | convolution fusion | flops 547356672 | bytes 9970688 | tf_op jit(solution)/shard_map/while/body/eval_jaxpr/gqn,nd->gqd/dot_general | solution.py:31
  117.3 2.6 fusion.59
  119.9 2.0 convert_reduce_fusion.3
  122.5 4.5 %fusion.60 = f32[8,8,256,128]{3,2,1,0:T(8,128)} fusion(f32[8,8,256,128]{3,2,1,0:T(8,128)} %get-tuple-element.319, s32[]{:T(128)S(6)} %copy.81, bf16[8,1024,128]{1,2,0:T(8,128)(2,1)} %get-tuple-element.332, f32[1024,256,8]{1,0,2:T(8,128)S(1)} %get-tuple-element.303, f32[8,256]{1,0:T(8,128)S(1)} %get-tuple-element.302, ...), kind=kOutput, calls=%fused_computation.15.clone.1 | convolution fusion | flops 547356672 | bytes 9970688 | tf_op jit(solution)/shard_map/while/body/eval_jaxpr/gqn,nd->gqd/dot_general | solution.py:31
  127.0 3.3 all-to-all-start.2
  130.3 4.1 %all-to-all-done.2 = f32[4,16,256]{2,1,0:T(8,128)S(1)} async-done(((f32[4,16,256]{2,1,0:T(8,128)}), f32[4,16,256]{2,1,0:T(8,128)S(1)}, u32[]{:S(2)}, u32[]{:S(2)}) %all-to-all-start.2) | async-done | bytes 65568 | tf_op jit(solution)/shard_map/all_to_all | solution.py:93
  135.0 3.3 all-to-all-start.1
  138.3 4.1 %all-to-all-done.1 = f32[4,16,256]{2,1,0:T(8,128)S(1)} async-done(((f32[4,16,256]{2,1,0:T(8,128)}), f32[4,16,256]{2,1,0:T(8,128)S(1)}, u32[]{:S(2)}, u32[]{:S(2)}) %all-to-all-start.1) | async-done | bytes 65568 | tf_op jit(solution)/shard_map/all_to_all | solution.py:92
  143.0 5.7 %all-to-all-start = ((f32[4,16,256,128]{3,2,1,0:T(8,128)}), f32[4,16,256,128]{3,2,1,0:T(8,128)}, u32[]{:S(2)}, u32[]{:S(2)}) async-start(f32[4,16,256,128]{3,2,1,0:T(8,128)} %bitcast.131), calls=%async_computation | async-start | bytes 16777216 | tf_op jit(solution)/shard_map/all_to_all | solution.py:94
  148.8 32.8 %all-gather = bf16[8,2,8192]{2,1,0:T(2,128)(2,1)} all-gather(bf16[1,2,8192]{2,1,0:T(2,128)(2,1)S(1)} %dynamic-slice_bitcast_fusion), channel_id=1, replica_groups=mesh['group'=8,'tp'=4] {'group'}, dimensions={0}, use_global_device_ids=true | all-gather | bytes 294912 | tf_op jit(solution)/shard_map/all_gather | solution.py:115
  185.8 56.9 %all_gather.26 = f32[4,3,64]{2,1,0:T(4,128)S(1)} all-gather(f32[1,3,64]{2,1,0:T(4,128)S(1)} %all_gather_reshape.9), channel_id=1, replica_groups=mesh['group'=8,'tp'=4] {'tp'}, dimensions={0}, use_global_device_ids=true | all-gather | bytes 3840 | tf_op jit(solution)/shard_map/all_gather | solution.py:13
  242.7 5.1 %all_gather.27 = f32[4,3,64]{2,1,0:T(4,128)S(1)} all-gather(f32[1,3,64]{2,1,0:T(4,128)S(1)} %all_gather_reshape.10), channel_id=1, replica_groups=mesh['group'=8,'tp'=4] {'tp'}, dimensions={0}, use_global_device_ids=true | all-gather | bytes 3840 | tf_op jit(solution)/shard_map/all_gather | solution.py:13
  247.8 2.8 convolution_bitcast_fusion.1
  250.7 6.5 %all_gather.28 = f32[4,3,64,128]{3,2,1,0:T(8,128)S(1)} all-gather(f32[1,3,64,128]{3,2,1,0:T(8,128)S(1)} %convolution_bitcast_fusion.1), channel_id=1, replica_groups=mesh['group'=8,'tp'=4] {'tp'}, dimensions={0}, use_global_device_ids=true | all-gather | bytes 491520 | tf_op jit(solution)/shard_map/all_gather | solution.py:13
  257.9 26.2 %all-gather.2 = f32[8,3,16]{2,1,0:T(4,128)S(1)} all-gather(f32[1,3,16]{2,1,0:T(4,128)S(1)} %dynamic-slice_bitcast_fusion.1), channel_id=1, replica_groups=mesh['group'=8,'tp'=4] {'group'}, dimensions={0}, use_global_device_ids=true | all-gather | bytes 1728 | tf_op jit(solution)/shard_map/all_gather | solution.py:147
  284.3 26.0 %all-gather.1 = f32[8,3,16]{2,1,0:T(4,128)S(1)} all-gather(f32[1,3,16]{2,1,0:T(4,128)S(1)} %dynamic-slice_bitcast_fusion.2), channel_id=1, replica_groups=mesh['group'=8,'tp'=4] {'group'}, dimensions={0}, use_global_device_ids=true | all-gather | bytes 1728 | tf_op jit(solution)/shard_map/all_gather | solution.py:146
  310.4 30.6 %all_gather.29 = f32[24,16,128]{2,1,0:T(8,128)S(1)} all-gather(f32[3,16,128]{2,1,0:T(8,128)S(1)} %constant_dynamic-slice_fusion), channel_id=1, replica_groups=mesh['group'=8,'tp'=4] {'group'}, dimensions={0}, use_global_device_ids=true | all-gather | bytes 221184 | tf_op jit(solution)/shard_map/all_gather | solution.py:148
  343.7 5.4 %multiply_reduce_fusion = f32[16,256,128]{2,1,0:T(8,128)S(1)} fusion(f32[4,16,256,128]{3,2,1,0:T(8,128)} %all-to-all-done, f32[4,16,256]{2,1,0:T(8,128)S(1)} %get-tuple-element.181), kind=kLoop, calls=%fused_computation.28 | loop fusion | flops 3670016 | bytes 10551296 | tf_op jit(solution)/shard_map/reduce_sum | solution.py:41
  (96 shorter events, 24.8 us)
Async XLA Ops:
  7.2 40.4 %all-gather.5.cloned.1.call-start = ((), (), s32[]{:S(2)}) async-start(), calls=%async_computation.3 | async-start | bytes 5242880 | tf_op jit(solution)/shard_map/all_gather | solution.py:78
  9.5 12.4 %collective-permute-start = (bf16[2,2048]{1,0:T(2,128)(2,1)}, bf16[2,2048]{1,0:T(2,128)(2,1)S(1)}, u32[]{:S(2)}, u32[]{:S(2)}) collective-permute-start(bf16[2,2048]{1,0:T(2,128)(2,1)} %param.14), channel_id=1, source_target_pairs={{0,1},{1,2},{2,3},{3,0},{4,5},{5,6},{6,7},{7,4},{8,9},{9,10},{10,1... | collective-permute-start | bytes 24584 | tf_op jit(solution)/shard_map/ppermute | solution.py:108
  10.0 7.7 %copy-start = (bf16[3,2,512,1024]{3,2,1,0:T(8,128)(2,1)S(1)}, bf16[3,2,512,1024]{3,2,1,0:T(8,128)(2,1)}, u32[]{:S(2)}) copy-start(bf16[3,2,512,1024]{3,2,1,0:T(8,128)(2,1)} %param.15) | copy-start | bytes 18874372
  17.7 3.5 copy-start.7
  21.9 17.7 %collective-permute-start.1 = (bf16[2,2048]{1,0:T(2,128)(2,1)S(1)}, bf16[2,2048]{1,0:T(2,128)(2,1)S(1)}, u32[]{:S(2)}, u32[]{:S(2)}) collective-permute-start(bf16[2,2048]{1,0:T(2,128)(2,1)S(1)} %collective-permute-done), channel_id=1, source_target_pairs={{0,1},{1,2},{2,3},{3,0},{4,5},{5,6},{6,7},{7,4},{8,9},{9,10},{10,1... | collective-permute-start | bytes 24584 | tf_op jit(solution)/shard_map/ppermute | solution.py:108
  39.6 90.6 %collective-permute-start.2 = (bf16[2,2048]{1,0:T(2,128)(2,1)S(1)}, bf16[2,2048]{1,0:T(2,128)(2,1)S(1)}, u32[]{:S(2)}, u32[]{:S(2)}) collective-permute-start(bf16[2,2048]{1,0:T(2,128)(2,1)S(1)} %collective-permute-done.1), channel_id=1, source_target_pairs={{0,1},{1,2},{2,3},{3,0},{4,5},{5,6},{6,7},{7,4},{8,9},{9,10},{10,1... | collective-permute-start | bytes 24584 | tf_op jit(solution)/shard_map/ppermute | solution.py:108
  127.0 7.4 %all-to-all-start.2 = ((f32[4,16,256]{2,1,0:T(8,128)}), f32[4,16,256]{2,1,0:T(8,128)S(1)}, u32[]{:S(2)}, u32[]{:S(2)}) async-start(f32[4,16,256]{2,1,0:T(8,128)} %bitcast.13), calls=%async_computation.2 | async-start | bytes 131072 | tf_op jit(solution)/shard_map/all_to_all | solution.py:93
  134.3 0.6 copy-start.3
  135.0 7.4 %all-to-all-start.1 = ((f32[4,16,256]{2,1,0:T(8,128)}), f32[4,16,256]{2,1,0:T(8,128)S(1)}, u32[]{:S(2)}, u32[]{:S(2)}) async-start(f32[4,16,256]{2,1,0:T(8,128)} %bitcast.11), calls=%async_computation.1 | async-start | bytes 131072 | tf_op jit(solution)/shard_map/all_to_all | solution.py:92
  142.4 0.6 copy-start.1
  142.4 6.3 %copy-start.5 = (bf16[2,2048]{1,0:T(2,128)(2,1)S(1)}, bf16[2,2048]{1,0:T(2,128)(2,1)}, u32[]{:S(2)}) copy-start(bf16[2,2048]{1,0:T(2,128)(2,1)} %param.14) | copy-start | bytes 24580
  143.0 200.7 %all-to-all-start = ((f32[4,16,256,128]{3,2,1,0:T(8,128)}), f32[4,16,256,128]{3,2,1,0:T(8,128)}, u32[]{:S(2)}, u32[]{:S(2)}) async-start(f32[4,16,256,128]{3,2,1,0:T(8,128)} %bitcast.131), calls=%async_computation | async-start | bytes 16777216 | tf_op jit(solution)/shard_map/all_to_all | solution.py:94
  185.4 157.3 %copy-start.6 = (pred[2,24]{1,0:T(4,128)(4,1)S(1)}, pred[2,24]{1,0:T(4,128)(4,1)}, u32[]{:S(2)}) copy-start(pred[2,24]{1,0:T(4,128)(4,1)} %broadcast_compare_fusion.2) | copy-start | bytes 148
  185.4 158.3 %copy-start.2 = (f32[4,16,256]{2,1,0:T(8,128)S(1)}, f32[4,16,256]{2,1,0:T(8,128)}, u32[]{:S(2)}) copy-start(f32[4,16,256]{2,1,0:T(8,128)} %copy-done.1) | copy-start | bytes 196612
  185.4 158.3 %copy-start.4 = (f32[4,16,256]{2,1,0:T(8,128)S(1)}, f32[4,16,256]{2,1,0:T(8,128)}, u32[]{:S(2)}) copy-start(f32[4,16,256]{2,1,0:T(8,128)} %copy-done.3) | copy-start | bytes 196612
Sparse Core Ops, SparseCore 0:
  10.1 37.3 all-gather.4
